TPU v7x, 32 devices: a whole 2x2x4 slice. The times are simulated.
32 devices in a mesh: seg: 16 (over z, y, x), samp: 2 (over core).
Axes of the slice: x: 2, y: 2, z: 4, core: 2. Of those that a mesh axis runs over, the one named last changes fastest.
Arguments:
- rigidity_diagonal_cells: bfloat16 [512, 128, 128], P('seg')
- rigidity_lower_cells: bfloat16 [512, 128, 128], P('seg'), may hold values from -0.5 to 0.5
- inverse_diagonal_cells: bfloat16 [512, 128, 128], P('seg')
- bedding_rigidity_per_unknown: float32 [512, 128], P('seg'), may hold values from 0.3 to 2
- bedding_regime: int32 [512], P('seg'), may hold values from 0 to 2
- dilation_push_per_kelvin: float32 [512, 128], P('seg'), may hold values from 1 to 16
- heat_shape_functions: bfloat16 [512, 512], P('seg'), may hold values from -0.25 to 0.25
- sampled_shape_weights: bfloat16 [64, 512], P('samp'), may hold values from -6 to 6
- joined_segment_table: int32 [16, 2], P('seg'), may hold values from 0 to 15
- joint_rigidity: float32 [16, 2], P('seg'), may hold values from 1.2 to 3.6
Outputs:
- displacement: float32 [64, 512, 128], P('samp', 'seg')
- kl_grad: float32 [512], replicated
Inputs may be any that keep to these rules, and one draw needn't show every extreme that they name: `joined_segment_table`: every entry names a segment.
All inputs are finite; a program needn't handle non-finite values.
Results may differ from a plain program's by a relative error of at most 0.013.
Values may be sent and summed in bfloat16 or wider, within the bound.
A program may use at most 64 MiB of HBM per device.

v0:
```python
import math
import jax
import jax.numpy as jnp
from jax import lax
from jax.sharding import PartitionSpec as P

STEPS = 4


def shifted(value, axis, steps):
    count = lax.axis_size(axis)
    first, last = (max(0, -steps), min(count, count - steps))
    return lax.ppermute(value, axis, [(source, source + steps) for source in range(first, last)])


def stiffness(
    field_round, rigidity_diagonal_cells, rigidity_lower_cells, joined_segment_table, joint_rigidity
):
    own_term = jnp.einsum(
        "sjb,jab->sja", field_round, rigidity_diagonal_cells, preferred_element_type=jnp.float32
    )
    upward = jnp.einsum(
        "sjb,jba->sja", field_round, rigidity_lower_cells, preferred_element_type=jnp.float32
    ).astype(jnp.bfloat16)
    below_rim = shifted(field_round[:, -1:, :], "seg", 1)
    above_rim = shifted(upward[:, :1, :], "seg", -1)
    interfaces = lax.all_gather(field_round[:, :1, :], "seg", axis=1, tiled=True)
    lower_field = jnp.concatenate([below_rim, field_round[:, :-1]], axis=1)
    below_term = jnp.einsum(
        "sjb,jab->sja", lower_field, rigidity_lower_cells, preferred_element_type=jnp.float32
    )
    upper_term = jnp.concatenate([upward[:, 1:], above_rim], axis=1).astype(jnp.float32)
    result = own_term + below_term + upper_term
    partner = jnp.take(interfaces, joined_segment_table[0], axis=1).astype(jnp.float32)
    own_interface = field_round[:, 0:1, :].astype(jnp.float32)
    spring = jnp.sum(joint_rigidity[0][None, :, None] * (own_interface - partner), axis=1)
    return result.at[:, 0, :].add(spring)


def ballast(state, bedding_rigidity_per_unknown, bedding_regime):
    code = bedding_regime[None, :, None]
    stiff = bedding_rigidity_per_unknown[None]
    magnitude = 1.0 + jnp.abs(state)
    slide = jnp.tanh(state)
    force = jnp.where(
        code == 0, stiff * state, jnp.where(code == 1, stiff * state / magnitude, stiff * slide)
    )
    tangent = jnp.where(
        code == 0,
        stiff + 0.0 * state,
        jnp.where(code == 1, stiff / (magnitude * magnitude), stiff * (1.0 - slide * slide)),
    )
    return (force, tangent)


def blockwise(inverse_diagonal_cells, field_round):
    return jnp.einsum(
        "jab,sjb->sja", inverse_diagonal_cells, field_round, preferred_element_type=jnp.float32
    )


def body(
    rigidity_diagonal_cells,
    rigidity_lower_cells,
    inverse_diagonal_cells,
    bedding_rigidity_per_unknown,
    bedding_regime,
    dilation_push_per_kelvin,
    heat_shape_functions,
    sampled_shape_weights,
    joined_segment_table,
    joint_rigidity,
):
    samples_here = sampled_shape_weights.shape[0]
    blocks_here = rigidity_diagonal_cells.shape[0]
    width = rigidity_diagonal_cells.shape[1]
    shape_functions = heat_shape_functions.shape[1]
    complete_shape_functions = heat_shape_functions.astype(jnp.float32)
    heat_distribution = jnp.dot(
        sampled_shape_weights, heat_shape_functions.T, preferred_element_type=jnp.float32
    )
    heat_driven_source = dilation_push_per_kelvin[None] * heat_distribution[:, :, None]
    state = jnp.zeros((samples_here, blocks_here, width), jnp.float32)
    grad_total = jnp.zeros((shape_functions,), jnp.float32)
    for iteration in range(STEPS):
        state_round = state.astype(jnp.bfloat16)
        force, tangent = ballast(state, bedding_rigidity_per_unknown, bedding_regime)
        residual_vector = (
            heat_driven_source
            - stiffness(
                state_round,
                rigidity_diagonal_cells,
                rigidity_lower_cells,
                joined_segment_table,
                joint_rigidity,
            )
            - force
        )
        initial_newton_step = blockwise(
            inverse_diagonal_cells, residual_vector.astype(jnp.bfloat16)
        )
        second = (
            residual_vector
            - stiffness(
                initial_newton_step.astype(jnp.bfloat16),
                rigidity_diagonal_cells,
                rigidity_lower_cells,
                joined_segment_table,
                joint_rigidity,
            )
            - tangent * initial_newton_step
        )
        state = (
            state
            + initial_newton_step
            + blockwise(inverse_diagonal_cells, second.astype(jnp.bfloat16))
        )
        adjoint = jnp.einsum(
            "sja,jab->sjb",
            state.astype(jnp.bfloat16),
            inverse_diagonal_cells,
            preferred_element_type=jnp.float32,
        )
        weighted = jnp.sum(jnp.sum(dilation_push_per_kelvin[None] * adjoint, axis=2), axis=0)
        partial_value = jnp.dot(weighted, complete_shape_functions, precision=lax.Precision.HIGHEST)
        grad_total = grad_total + lax.psum(partial_value, ("seg", "samp"))
    every_block_list = blocks_here * lax.axis_size("seg")
    all_samples = samples_here * lax.axis_size("samp")
    scale = math.sqrt(shape_functions / (every_block_list * all_samples * width))
    return (state, grad_total * scale)


def solution(mesh):
    placed = (
        P("seg", None, None),
        P("seg", None, None),
        P("seg", None, None),
        P("seg", None),
        P("seg"),
        P("seg", None),
        P("seg", None),
        P("samp", None),
        P("seg", None),
        P("seg", None),
    )
    return jax.shard_map(
        body, mesh=mesh, in_specs=placed, out_specs=(P("samp", "seg", None), P()), check_vma=False
    )
```

profile of v0, /device:TPU:14, one launch (start us, length us, event | category | flops | bytes accessed | tf_op | source)
XLA Modules:
  0.0 460.8 jit_solution(1154479130879753834)
XLA Ops:
  0.7 3.5 collective-permute-start
  4.6 2.6 collective-permute-start.1
  17.6 4.8 %collective-permute-start.2 = (bf16[32,1,128]{2,0,1:T(8,128)(2,1)}, bf16[32,1,128]{2,0,1:T(8,128)(2,1)}, u32[]{:S(2)}, u32[]{:S(2)}) collective-permute-start(bf16[32,1,128]{2,0,1:T(8,128)(2,1)} %get-tuple-element.125), channel_id=1, source_target_pairs={{0,2},{2,4},{4,6},{6,8},{8,10},{10,12},{12,14},{14,16},{16,18},{18... | collective-permute-start | bytes 24584 | tf_op jit(solution)/shard_map/ppermute | solution.py:13
  22.4 30.9 %all_gather.22 = bf16[32,16,128]{2,0,1:T(8,128)(2,1)} all-gather(bf16[32,1,128]{2,0,1:T(8,128)(2,1)S(1)} %get-tuple-element.124), channel_id=1, replica_groups=mesh['seg'=16,'samp'=2] {'seg'}, dimensions={1}, use_global_device_ids=true | all-gather | bytes 139264 | tf_op jit(solution)/shard_map/all_gather | solution.py:27
  55.5 3.5 collective-permute-start.3
  59.1 4.1 collective-permute-done.3
  69.9 3.9 collective-permute-start.4
  73.8 34.6 %all_gather.23 = bf16[32,16,128]{2,0,1:T(8,128)(2,1)} all-gather(bf16[32,1,128]{2,0,1:T(8,128)(2,1)S(1)} %get-tuple-element.121), channel_id=1, replica_groups=mesh['seg'=16,'samp'=2] {'seg'}, dimensions={1}, use_global_device_ids=true | all-gather | bytes 139264 | tf_op jit(solution)/shard_map/all_gather | solution.py:27
  110.5 1.9 collective-permute-start.5
  112.6 5.3 %collective-permute-done.5 = bf16[32,1,128]{2,0,1:T(8,128)(2,1)S(1)} collective-permute-done((bf16[32,1,128]{2,0,1:T(8,128)(2,1)S(1)}, bf16[32,1,128]{2,0,1:T(8,128)(2,1)S(1)}, u32[]{:S(2)}, u32[]{:S(2)}) %collective-permute-start.5) | collective-permute-done | bytes 8224 | tf_op jit(solution)/shard_map/ppermute | solution.py:13
  124.6 1.9 collective-permute-start.6
  126.5 40.1 %all_gather.24 = bf16[32,16,128]{2,0,1:T(8,128)(2,1)} all-gather(bf16[32,1,128]{2,0,1:T(8,128)(2,1)S(1)} %get-tuple-element.118), channel_id=1, replica_groups=mesh['seg'=16,'samp'=2] {'seg'}, dimensions={1}, use_global_device_ids=true | all-gather | bytes 139264 | tf_op jit(solution)/shard_map/all_gather | solution.py:27
  168.8 1.9 collective-permute-start.7
  170.9 5.2 %collective-permute-done.7 = bf16[32,1,128]{2,0,1:T(8,128)(2,1)S(1)} collective-permute-done((bf16[32,1,128]{2,0,1:T(8,128)(2,1)S(1)}, bf16[32,1,128]{2,0,1:T(8,128)(2,1)S(1)}, u32[]{:S(2)}, u32[]{:S(2)}) %collective-permute-start.7) | collective-permute-done | bytes 8224 | tf_op jit(solution)/shard_map/ppermute | solution.py:13
  178.2 1.6 fusion.135
  184.1 1.9 collective-permute-start.8
  186.0 40.2 %all_gather.25 = bf16[32,16,128]{2,0,1:T(8,128)(2,1)} all-gather(bf16[32,1,128]{2,0,1:T(8,128)(2,1)S(1)} %get-tuple-element.115), channel_id=1, replica_groups=mesh['seg'=16,'samp'=2] {'seg'}, dimensions={1}, use_global_device_ids=true | all-gather | bytes 139264 | tf_op jit(solution)/shard_map/all_gather | solution.py:27
  228.4 1.9 collective-permute-start.9
  230.5 5.3 %collective-permute-done.9 = bf16[32,1,128]{2,0,1:T(8,128)(2,1)S(1)} collective-permute-done((bf16[32,1,128]{2,0,1:T(8,128)(2,1)S(1)}, bf16[32,1,128]{2,0,1:T(8,128)(2,1)S(1)}, u32[]{:S(2)}, u32[]{:S(2)}) %collective-permute-start.9) | collective-permute-done | bytes 8224 | tf_op jit(solution)/shard_map/ppermute | solution.py:13
  242.5 1.9 collective-permute-start.10
  244.4 40.1 %all_gather.26 = bf16[32,16,128]{2,0,1:T(8,128)(2,1)} all-gather(bf16[32,1,128]{2,0,1:T(8,128)(2,1)S(1)} %get-tuple-element.112), channel_id=1, replica_groups=mesh['seg'=16,'samp'=2] {'seg'}, dimensions={1}, use_global_device_ids=true | all-gather | bytes 139264 | tf_op jit(solution)/shard_map/all_gather | solution.py:27
  286.6 2.1 collective-permute-start.11
  288.9 5.0 %collective-permute-done.11 = bf16[32,1,128]{2,0,1:T(8,128)(2,1)S(1)} collective-permute-done((bf16[32,1,128]{2,0,1:T(8,128)(2,1)S(1)}, bf16[32,1,128]{2,0,1:T(8,128)(2,1)S(1)}, u32[]{:S(2)}, u32[]{:S(2)}) %collective-permute-start.11) | collective-permute-done | bytes 8224 | tf_op jit(solution)/shard_map/ppermute | solution.py:13
  301.9 1.9 collective-permute-start.12
  303.9 40.1 %all_gather.27 = bf16[32,16,128]{2,0,1:T(8,128)(2,1)} all-gather(bf16[32,1,128]{2,0,1:T(8,128)(2,1)S(1)} %get-tuple-element.109), channel_id=1, replica_groups=mesh['seg'=16,'samp'=2] {'seg'}, dimensions={1}, use_global_device_ids=true | all-gather | bytes 139264 | tf_op jit(solution)/shard_map/all_gather | solution.py:27
  346.1 2.0 collective-permute-start.13
  348.2 5.2 %collective-permute-done.13 = bf16[32,1,128]{2,0,1:T(8,128)(2,1)S(1)} collective-permute-done((bf16[32,1,128]{2,0,1:T(8,128)(2,1)S(1)}, bf16[32,1,128]{2,0,1:T(8,128)(2,1)S(1)}, u32[]{:S(2)}, u32[]{:S(2)}) %collective-permute-start.13) | collective-permute-done | bytes 8224 | tf_op jit(solution)/shard_map/ppermute | solution.py:13
  359.6 1.9 collective-permute-start.14
  361.5 37.3 %all_gather.28 = bf16[32,16,128]{2,0,1:T(8,128)(2,1)S(1)} all-gather(bf16[32,1,128]{2,0,1:T(8,128)(2,1)S(1)} %get-tuple-element.106), channel_id=1, replica_groups=mesh['seg'=16,'samp'=2] {'seg'}, dimensions={1}, use_global_device_ids=true | all-gather | bytes 139264 | tf_op jit(solution)/shard_map/all_gather | solution.py:27
  400.1 2.0 collective-permute-start.15
  402.2 5.2 %collective-permute-done.15 = bf16[32,1,128]{2,0,1:T(8,128)(2,1)S(1)} collective-permute-done((bf16[32,1,128]{2,0,1:T(8,128)(2,1)S(1)}, bf16[32,1,128]{2,0,1:T(8,128)(2,1)S(1)}, u32[]{:S(2)}, u32[]{:S(2)}) %collective-permute-start.15) | collective-permute-done | bytes 8224 | tf_op jit(solution)/shard_map/ppermute | solution.py:13
  412.1 48.0 %psum.34 = f32[512]{0:T(512)S(1)} all-reduce(f32[512]{0:T(512)S(1)} %add_add_fusion), channel_id=1, replica_groups=mesh['seg'=16,'samp'=2] {'seg','samp'}, use_global_device_ids=true, to_apply=%region_9.11 | all-reduce | flops 512 | bytes 4096 | tf_op jit(solution)/shard_map/psum | solution.py:126
  (226 shorter events, 71.2 us)
Async XLA Ops:
  0.6 7.8 %copy-start.1 = (bf16[32,128,128]{2,1,0:T(8,128)(2,1)S(1)}, bf16[32,128,128]{2,1,0:T(8,128)(2,1)}, u32[]{:S(2)}) copy-start(bf16[32,128,128]{2,1,0:T(8,128)(2,1)} %param.28) | copy-start | bytes 3145732
  0.7 10.2 %collective-permute-start = (bf16[32,1,128]{2,0,1:T(8,128)(2,1)S(1)}, bf16[32,1,128]{2,0,1:T(8,128)(2,1)S(1)}, u32[]{:S(2)}, u32[]{:S(2)}) collective-permute-start(bf16[32,1,128]{2,0,1:T(8,128)(2,1)S(1)} %slice.302), channel_id=1, source_target_pairs={{0,2},{2,4},{4,6},{6,8},{8,10},{10,12},{12,14},{14,16},{16,18},{18... | collective-permute-start | bytes 24584 | tf_op jit(solution)/shard_map/ppermute | solution.py:13
  4.6 7.5 %collective-permute-start.1 = (bf16[32,1,128]{2,0,1:T(8,128)(2,1)S(1)}, bf16[32,1,128]{2,0,1:T(8,128)(2,1)S(1)}, u32[]{:S(2)}, u32[]{:S(2)}) collective-permute-start(bf16[32,1,128]{2,0,1:T(8,128)(2,1)S(1)} %slice.366), channel_id=1, source_target_pairs={{2,0},{4,2},{6,4},{8,6},{10,8},{12,10},{14,12},{16,14},{18,16},{20... | collective-permute-start | bytes 24584 | tf_op jit(solution)/shard_map/ppermute | solution.py:13
  14.3 44.7 %copy-start.7 = (bf16[32,32,128]{2,0,1:T(8,128)(2,1)}, bf16[32,32,128]{2,0,1:T(8,128)(2,1)S(1)}, u32[]{:S(2)}) copy-start(bf16[32,32,128]{2,0,1:T(8,128)(2,1)S(1)} %convert_bitcast_fusion) | copy-start | bytes 786436
  17.6 41.5 %collective-permute-start.2 = (bf16[32,1,128]{2,0,1:T(8,128)(2,1)}, bf16[32,1,128]{2,0,1:T(8,128)(2,1)}, u32[]{:S(2)}, u32[]{:S(2)}) collective-permute-start(bf16[32,1,128]{2,0,1:T(8,128)(2,1)} %get-tuple-element.125), channel_id=1, source_target_pairs={{0,2},{2,4},{4,6},{6,8},{8,10},{10,12},{12,14},{14,16},{16,18},{18... | collective-permute-start | bytes 24584 | tf_op jit(solution)/shard_map/ppermute | solution.py:13
  55.5 7.7 %collective-permute-start.3 = (bf16[32,1,128]{2,0,1:T(8,128)(2,1)S(1)}, bf16[32,1,128]{2,0,1:T(8,128)(2,1)S(1)}, u32[]{:S(2)}, u32[]{:S(2)}) collective-permute-start(bf16[32,1,128]{2,0,1:T(8,128)(2,1)S(1)} %slice.371), channel_id=1, source_target_pairs={{2,0},{4,2},{6,4},{8,6},{10,8},{12,10},{14,12},{16,14},{18,16},{20... | collective-permute-start | bytes 24584 | tf_op jit(solution)/shard_map/ppermute | solution.py:13
  59.1 5.5 %copy-start.4 = (f32[32,32,128]{2,0,1:T(8,128)S(1)}, f32[32,32,128]{2,0,1:T(8,128)}, u32[]{:S(2)}) copy-start(f32[32,32,128]{2,0,1:T(8,128)} %copy-done.3) | copy-start | bytes 1572868
  59.1 5.5 %copy-start.6 = (f32[32,32,128]{2,1,0:T(8,128)S(1)}, f32[32,32,128]{2,1,0:T(8,128)}, u32[]{:S(2)}) copy-start(f32[32,32,128]{2,1,0:T(8,128)} %copy-done.5) | copy-start | bytes 1572868
  69.9 42.7 %collective-permute-start.4 = (bf16[32,1,128]{2,0,1:T(8,128)(2,1)}, bf16[32,1,128]{2,0,1:T(8,128)(2,1)}, u32[]{:S(2)}, u32[]{:S(2)}) collective-permute-start(bf16[32,1,128]{2,0,1:T(8,128)(2,1)} %get-tuple-element.122), channel_id=1, source_target_pairs={{0,2},{2,4},{4,6},{6,8},{8,10},{10,12},{12,14},{14,16},{16,18},{18... | collective-permute-start | bytes 24584 | tf_op jit(solution)/shard_map/ppermute | solution.py:13
  110.5 7.3 %collective-permute-start.5 = (bf16[32,1,128]{2,0,1:T(8,128)(2,1)S(1)}, bf16[32,1,128]{2,0,1:T(8,128)(2,1)S(1)}, u32[]{:S(2)}, u32[]{:S(2)}) collective-permute-start(bf16[32,1,128]{2,0,1:T(8,128)(2,1)S(1)} %slice.377), channel_id=1, source_target_pairs={{2,0},{4,2},{6,4},{8,6},{10,8},{12,10},{14,12},{16,14},{18,16},{20... | collective-permute-start | bytes 24584 | tf_op jit(solution)/shard_map/ppermute | solution.py:13
  112.6 6.7 %copy-start.24 = (f32[32,32,128]{2,0,1:T(8,128)S(1)}, f32[32,32,128]{2,0,1:T(8,128)}, u32[]{:S(2)}) copy-start(f32[32,32,128]{2,0,1:T(8,128)} %get-tuple-element.129) | copy-start | bytes 1572868
  124.6 46.3 %collective-permute-start.6 = (bf16[32,1,128]{2,0,1:T(8,128)(2,1)}, bf16[32,1,128]{2,0,1:T(8,128)(2,1)}, u32[]{:S(2)}, u32[]{:S(2)}) collective-permute-start(bf16[32,1,128]{2,0,1:T(8,128)(2,1)} %get-tuple-element.119), channel_id=1, source_target_pairs={{0,2},{2,4},{4,6},{6,8},{8,10},{10,12},{12,14},{14,16},{16,18},{18... | collective-permute-start | bytes 24584 | tf_op jit(solution)/shard_map/ppermute | solution.py:13
  168.8 7.3 %collective-permute-start.7 = (bf16[32,1,128]{2,0,1:T(8,128)(2,1)S(1)}, bf16[32,1,128]{2,0,1:T(8,128)(2,1)S(1)}, u32[]{:S(2)}, u32[]{:S(2)}) collective-permute-start(bf16[32,1,128]{2,0,1:T(8,128)(2,1)S(1)} %slice.383), channel_id=1, source_target_pairs={{2,0},{4,2},{6,4},{8,6},{10,8},{12,10},{14,12},{16,14},{18,16},{20... | collective-permute-start | bytes 24584 | tf_op jit(solution)/shard_map/ppermute | solution.py:13
  170.8 6.7 %copy-start.19 = (f32[32,32,128]{2,0,1:T(8,128)S(1)}, f32[32,32,128]{2,0,1:T(8,128)}, u32[]{:S(2)}) copy-start(f32[32,32,128]{2,0,1:T(8,128)} %copy-done.18) | copy-start | bytes 1572868
  170.9 6.7 %copy-start.25 = (f32[32,32,128]{2,0,1:T(8,128)S(1)}, f32[32,32,128]{2,0,1:T(8,128)}, u32[]{:S(2)}) copy-start(f32[32,32,128]{2,0,1:T(8,128)} %get-tuple-element.129) | copy-start | bytes 1572868
  170.9 6.7 %copy-start.50 = (f32[32,32,128]{2,0,1:T(8,128)S(1)}, f32[32,32,128]{2,0,1:T(8,128)}, u32[]{:S(2)}) copy-start(f32[32,32,128]{2,0,1:T(8,128)} %get-tuple-element.131) | copy-start | bytes 1572868
  184.1 46.4 %collective-permute-start.8 = (bf16[32,1,128]{2,0,1:T(8,128)(2,1)}, bf16[32,1,128]{2,0,1:T(8,128)(2,1)}, u32[]{:S(2)}, u32[]{:S(2)}) collective-permute-start(bf16[32,1,128]{2,0,1:T(8,128)(2,1)} %get-tuple-element.116), channel_id=1, source_target_pairs={{0,2},{2,4},{4,6},{6,8},{8,10},{10,12},{12,14},{14,16},{16,18},{18... | collective-permute-start | bytes 24584 | tf_op jit(solution)/shard_map/ppermute | solution.py:13
  228.4 7.3 %collective-permute-start.9 = (bf16[32,1,128]{2,0,1:T(8,128)(2,1)S(1)}, bf16[32,1,128]{2,0,1:T(8,128)(2,1)S(1)}, u32[]{:S(2)}, u32[]{:S(2)}) collective-permute-start(bf16[32,1,128]{2,0,1:T(8,128)(2,1)S(1)} %slice.389), channel_id=1, source_target_pairs={{2,0},{4,2},{6,4},{8,6},{10,8},{12,10},{14,12},{16,14},{18,16},{20... | collective-permute-start | bytes 24584 | tf_op jit(solution)/shard_map/ppermute | solution.py:13
  230.5 6.7 %copy-start.47 = (f32[32,32,128]{2,0,1:T(8,128)S(1)}, f32[32,32,128]{2,0,1:T(8,128)}, u32[]{:S(2)}) copy-start(f32[32,32,128]{2,0,1:T(8,128)} %get-tuple-element.133) | copy-start | bytes 1572868
  242.5 46.4 %collective-permute-start.10 = (bf16[32,1,128]{2,0,1:T(8,128)(2,1)}, bf16[32,1,128]{2,0,1:T(8,128)(2,1)}, u32[]{:S(2)}, u32[]{:S(2)}) collective-permute-start(bf16[32,1,128]{2,0,1:T(8,128)(2,1)} %get-tuple-element.113), channel_id=1, source_target_pairs={{0,2},{2,4},{4,6},{6,8},{8,10},{10,12},{12,14},{14,16},{16,18},{18... | collective-permute-start | bytes 24584 | tf_op jit(solution)/shard_map/ppermute | solution.py:13
  286.6 7.3 %collective-permute-start.11 = (bf16[32,1,128]{2,0,1:T(8,128)(2,1)S(1)}, bf16[32,1,128]{2,0,1:T(8,128)(2,1)S(1)}, u32[]{:S(2)}, u32[]{:S(2)}) collective-permute-start(bf16[32,1,128]{2,0,1:T(8,128)(2,1)S(1)} %slice.395), channel_id=1, source_target_pairs={{2,0},{4,2},{6,4},{8,6},{10,8},{12,10},{14,12},{16,14},{18,16},{20... | collective-permute-start | bytes 24584 | tf_op jit(solution)/shard_map/ppermute | solution.py:13
  288.9 6.5 %copy-start.21 = (f32[32,32,128]{2,0,1:T(8,128)S(1)}, f32[32,32,128]{2,0,1:T(8,128)}, u32[]{:S(2)}) copy-start(f32[32,32,128]{2,0,1:T(8,128)} %copy-done.20) | copy-start | bytes 1572868
  288.9 6.5 %copy-start.48 = (f32[32,32,128]{2,0,1:T(8,128)S(1)}, f32[32,32,128]{2,0,1:T(8,128)}, u32[]{:S(2)}) copy-start(f32[32,32,128]{2,0,1:T(8,128)} %get-tuple-element.133) | copy-start | bytes 1572868
  288.9 6.5 %copy-start.51 = (f32[32,32,128]{2,0,1:T(8,128)S(1)}, f32[32,32,128]{2,0,1:T(8,128)}, u32[]{:S(2)}) copy-start(f32[32,32,128]{2,0,1:T(8,128)} %get-tuple-element.135) | copy-start | bytes 1572868
  301.9 46.3 %collective-permute-start.12 = (bf16[32,1,128]{2,0,1:T(8,128)(2,1)}, bf16[32,1,128]{2,0,1:T(8,128)(2,1)}, u32[]{:S(2)}, u32[]{:S(2)}) collective-permute-start(bf16[32,1,128]{2,0,1:T(8,128)(2,1)} %get-tuple-element.110), channel_id=1, source_target_pairs={{0,2},{2,4},{4,6},{6,8},{8,10},{10,12},{12,14},{14,16},{16,18},{18... | collective-permute-start | bytes 24584 | tf_op jit(solution)/shard_map/ppermute | solution.py:13
  346.1 7.3 %collective-permute-start.13 = (bf16[32,1,128]{2,0,1:T(8,128)(2,1)S(1)}, bf16[32,1,128]{2,0,1:T(8,128)(2,1)S(1)}, u32[]{:S(2)}, u32[]{:S(2)}) collective-permute-start(bf16[32,1,128]{2,0,1:T(8,128)(2,1)S(1)} %slice.401), channel_id=1, source_target_pairs={{2,0},{4,2},{6,4},{8,6},{10,8},{12,10},{14,12},{16,14},{18,16},{20... | collective-permute-start | bytes 24584 | tf_op jit(solution)/shard_map/ppermute | solution.py:13
  348.2 6.7 %copy-start.45 = (f32[32,32,128]{2,0,1:T(8,128)S(1)}, f32[32,32,128]{2,0,1:T(8,128)}, u32[]{:S(2)}) copy-start(f32[32,32,128]{2,0,1:T(8,128)} %get-tuple-element.137) | copy-start | bytes 1572868
  359.6 42.6 %collective-permute-start.14 = (bf16[32,1,128]{2,0,1:T(8,128)(2,1)S(1)}, bf16[32,1,128]{2,0,1:T(8,128)(2,1)S(1)}, u32[]{:S(2)}, u32[]{:S(2)}) collective-permute-start(bf16[32,1,128]{2,0,1:T(8,128)(2,1)S(1)} %get-tuple-element.107), channel_id=1, source_target_pairs={{0,2},{2,4},{4,6},{6,8},{8,10},{10,12},{12,14},{14,16},{16,18},{18... | collective-permute-start | bytes 24584 | tf_op jit(solution)/shard_map/ppermute | solution.py:13
  400.1 7.3 %collective-permute-start.15 = (bf16[32,1,128]{2,0,1:T(8,128)(2,1)S(1)}, bf16[32,1,128]{2,0,1:T(8,128)(2,1)S(1)}, u32[]{:S(2)}, u32[]{:S(2)}) collective-permute-start(bf16[32,1,128]{2,0,1:T(8,128)(2,1)S(1)} %slice.407), channel_id=1, source_target_pairs={{2,0},{4,2},{6,4},{8,6},{10,8},{12,10},{14,12},{16,14},{18,16},{20... | collective-permute-start | bytes 24584 | tf_op jit(solution)/shard_map/ppermute | solution.py:13
  402.2 5.9 %copy-start.23 = (f32[32,32,128]{2,0,1:T(8,128)S(1)}, f32[32,32,128]{2,0,1:T(8,128)}, u32[]{:S(2)}) copy-start(f32[32,32,128]{2,0,1:T(8,128)} %copy-done.22) | copy-start | bytes 1572868
  402.2 5.9 %copy-start.46 = (f32[32,32,128]{2,0,1:T(8,128)S(1)}, f32[32,32,128]{2,0,1:T(8,128)}, u32[]{:S(2)}) copy-start(f32[32,32,128]{2,0,1:T(8,128)} %get-tuple-element.137) | copy-start | bytes 1572868
  402.2 5.9 %copy-start.49 = (f32[32,32,128]{2,0,1:T(8,128)S(1)}, f32[32,32,128]{2,0,1:T(8,128)}, u32[]{:S(2)}) copy-start(f32[32,32,128]{2,0,1:T(8,128)} %get-tuple-element.139) | copy-start | bytes 1572868
  (44 other events, 113.2 us)
where the time goes:
time: 462 us; the launch traced here: 461 us
  blocking collectives  311 us (67%)
  matrix products  43.6 us (9%)
  starting transfers between devices  39.7 us (9%)
  waiting for transfers between devices  36.5 us (8%)
  local copies, waits for them, and re-layouts  22.3 us (5%)
  other arithmetic  5.63 us (1%)
    all_gather x7, blocking collectives, stiffness(): lax.all_gather(field_round[:, :1, :], 'seg', axis=1, tiled=True)  263 us
    psum x1, blocking collectives, body(): grad_total = grad_total + lax.psum(partial_value, ('seg', 'samp'))  48 us
    ppermute x16, starting transfers between devices, shifted(): lax.ppermute(value, axis, [(source, source + steps) for source in range(f...  39.7 us
    ppermute x16, waiting for transfers between devices, shifted(): lax.ppermute(value, axis, [(source, source + steps) for source in range(f...  36.5 us
    dot_general x8, matrix products, stiffness(): jnp.einsum('sjb,jab->sja', field_round, rigidity_diagonal_cells, preferre...  11.7 us
    dot_general x8, matrix products, blockwise(): jnp.einsum('jab,sjb->sja', inverse_diagonal_cells, field_round, preferred...  10.8 us
    gather x8, local copies, waits for them, and re-layouts, stiffness(): jnp.take(interfaces, joined_segment_table[0], axis=1).astype(jnp.float32)  9.89 us
    dot_general x8, matrix products, stiffness(): jnp.einsum('sjb,jab->sja', lower_field, rigidity_lower_cells, preferred_e...  9.37 us
  transfers between devices with their start and end apart: 16, of which 8 were waited for; matrix products, arithmetic and copies ran while one was open for 4% of the time, Pallas kernels for 0%

commit v1 on v0

--- a/solution.py
+++ b/solution.py
@@ -1,3 +1,4 @@
+import functools
 import math
 import jax
 import jax.numpy as jnp
@@ -5,6 +6,15 @@
 from jax.sharding import PartitionSpec as P
 
 STEPS = 4
+
+
+def blocks_remake(field_in, link_axis):
+    carry = lax.all_gather(field_in, link_axis)
+    answer = jnp.sum(carry, 0)
+    return answer
+
+
+sides_edit = functools.partial(blocks_remake, link_axis=("seg", "samp"))
 
 
 def shifted(value, axis, steps):
@@ -123,7 +133,7 @@
         )
         weighted = jnp.sum(jnp.sum(dilation_push_per_kelvin[None] * adjoint, axis=2), axis=0)
         partial_value = jnp.dot(weighted, complete_shape_functions, precision=lax.Precision.HIGHEST)
-        grad_total = grad_total + lax.psum(partial_value, ("seg", "samp"))
+        grad_total = grad_total + sides_edit(partial_value)
     every_block_list = blocks_here * lax.axis_size("seg")
     all_samples = samples_here * lax.axis_size("samp")
     scale = math.sqrt(shape_functions / (every_block_list * all_samples * width))

time: 462 us -> 568 us (1.23)
  the two profiles are of different devices: /device:TPU:14 before, /device:TPU:0 now
where the time goes in v1:
time: 568 us; the launch traced here: 566 us
  blocking collectives  427 us (75%)
  matrix products  44.3 us (8%)
  starting transfers between devices  38.6 us (7%)
  local copies, waits for them, and re-layouts  28.2 us (5%)
  waiting for transfers between devices  16.6 us (3%)
  other arithmetic  10 us (2%)
    all_gather x7, blocking collectives, stiffness(): lax.all_gather(field_round[:, :1, :], 'seg', axis=1, tiled=True)  270 us
    all_gather x4, blocking collectives, blocks_remake(): carry = lax.all_gather(field_in, link_axis)  157 us
    ppermute x16, starting transfers between devices, shifted(): lax.ppermute(value, axis, [(source, source + steps) for source in range(f...  38.6 us
    ppermute x16, waiting for transfers between devices, shifted(): lax.ppermute(value, axis, [(source, source + steps) for source in range(f...  16.6 us
    dot_general x8, matrix products, stiffness(): jnp.einsum('sjb,jab->sja', field_round, rigidity_diagonal_cells, preferre...  11.6 us
  transfers between devices with their start and end apart: 16, of which 5 were waited for; matrix products, arithmetic and copies ran while one was open for 5% of the time, Pallas kernels for 0%

profile of v1, /device:TPU:0, one launch (start us, length us, event | category | flops | bytes accessed | tf_op | source)
XLA Modules:
  0.0 566.3 jit_solution(1376135916882519714)
XLA Ops:
  0.7 5.0 collective-permute-start
  17.6 5.1 collective-permute-start.2
  22.7 41.3 %all_gather.46 = bf16[32,16,128]{2,0,1:T(8,128)(2,1)} all-gather(bf16[32,1,128]{2,0,1:T(8,128)(2,1)S(1)} %get-tuple-element.124), channel_id=1, replica_groups=mesh['seg'=16,'samp'=2] {'seg'}, dimensions={1}, use_global_device_ids=true | all-gather | bytes 139264 | tf_op jit(solution)/shard_map/all_gather | solution.py:37
  63.9 1.6 gather_fusion.1
  67.8 4.1 collective-permute-done.3
  79.2 2.6 collective-permute-start.4
  81.8 38.5 %all_gather.47 = bf16[32,16,128]{2,0,1:T(8,128)(2,1)} all-gather(bf16[32,1,128]{2,0,1:T(8,128)(2,1)S(1)} %get-tuple-element.121), channel_id=1, replica_groups=mesh['seg'=16,'samp'=2] {'seg'}, dimensions={1}, use_global_device_ids=true | all-gather | bytes 139264 | tf_op jit(solution)/shard_map/all_gather | solution.py:37
  120.2 1.6 gather_fusion.2
  125.2 39.3 %all-gather.4 = f32[32,1,512]{2,1,0:T(1,128)S(1)} all-gather(f32[1,1,512]{2,1,0:T(1,128)S(1)} %copy-done.44), channel_id=2, replica_groups=mesh['seg'=16,'samp'=2] {'seg','samp'}, dimensions={0}, use_global_device_ids=true | all-gather | bytes 67584 | tf_op jit(solution)/shard_map/all_gather | solution.py:12
  166.2 1.8 fusion.9
  174.7 38.5 %all_gather.48 = bf16[32,16,128]{2,0,1:T(8,128)(2,1)} all-gather(bf16[32,1,128]{2,0,1:T(8,128)(2,1)S(1)} %get-tuple-element.118), channel_id=1, replica_groups=mesh['seg'=16,'samp'=2] {'seg'}, dimensions={1}, use_global_device_ids=true | all-gather | bytes 139264 | tf_op jit(solution)/shard_map/all_gather | solution.py:37
  213.1 1.6 gather_fusion.3
  217.0 4.1 collective-permute-done.7
  222.4 1.6 fusion.131
  228.4 5.4 collective-permute-start.8
  233.8 38.5 %all_gather.49 = bf16[32,16,128]{2,0,1:T(8,128)(2,1)} all-gather(bf16[32,1,128]{2,0,1:T(8,128)(2,1)S(1)} %get-tuple-element.115), channel_id=1, replica_groups=mesh['seg'=16,'samp'=2] {'seg'}, dimensions={1}, use_global_device_ids=true | all-gather | bytes 139264 | tf_op jit(solution)/shard_map/all_gather | solution.py:37
  272.2 1.6 gather_fusion.4
  277.1 39.3 %all-gather.5 = f32[32,1,512]{2,1,0:T(1,128)S(1)} all-gather(f32[1,1,512]{2,1,0:T(1,128)S(1)} %copy-done.45), channel_id=3, replica_groups=mesh['seg'=16,'samp'=2] {'seg','samp'}, dimensions={0}, use_global_device_ids=true | all-gather | bytes 67584 | tf_op jit(solution)/shard_map/all_gather | solution.py:12
  318.0 1.8 fusion.11
  326.5 38.5 %all_gather.50 = bf16[32,16,128]{2,0,1:T(8,128)(2,1)} all-gather(bf16[32,1,128]{2,0,1:T(8,128)(2,1)S(1)} %get-tuple-element.112), channel_id=1, replica_groups=mesh['seg'=16,'samp'=2] {'seg'}, dimensions={1}, use_global_device_ids=true | all-gather | bytes 139264 | tf_op jit(solution)/shard_map/all_gather | solution.py:37
  365.0 1.6 gather_fusion.5
  367.3 1.6 collective-permute-start.11
  369.1 3.9 collective-permute-done.11
  374.3 1.6 fusion.133
  380.2 5.4 collective-permute-start.12
  385.6 38.5 %all_gather.51 = bf16[32,16,128]{2,0,1:T(8,128)(2,1)} all-gather(bf16[32,1,128]{2,0,1:T(8,128)(2,1)S(1)} %get-tuple-element.109), channel_id=1, replica_groups=mesh['seg'=16,'samp'=2] {'seg'}, dimensions={1}, use_global_device_ids=true | all-gather | bytes 139264 | tf_op jit(solution)/shard_map/all_gather | solution.py:37
  424.1 1.6 gather_fusion.6
  428.9 39.3 %all-gather.6 = f32[32,1,512]{2,1,0:T(1,128)S(1)} all-gather(f32[1,1,512]{2,1,0:T(1,128)S(1)} %copy-done.46), channel_id=4, replica_groups=mesh['seg'=16,'samp'=2] {'seg','samp'}, dimensions={0}, use_global_device_ids=true | all-gather | bytes 67584 | tf_op jit(solution)/shard_map/all_gather | solution.py:12
  469.9 1.8 fusion.13
  478.4 36.1 %all_gather.52 = bf16[32,16,128]{2,0,1:T(8,128)(2,1)S(1)} all-gather(bf16[32,1,128]{2,0,1:T(8,128)(2,1)S(1)} %get-tuple-element.106), channel_id=1, replica_groups=mesh['seg'=16,'samp'=2] {'seg'}, dimensions={1}, use_global_device_ids=true | all-gather | bytes 139264 | tf_op jit(solution)/shard_map/all_gather | solution.py:37
  517.5 4.1 collective-permute-done.15
  525.6 39.4 %all-gather.7 = f32[32,1,512]{2,1,0:T(1,128)S(1)} all-gather(f32[1,1,512]{2,1,0:T(1,128)S(1)} %convolution_bitcast_fusion.6), channel_id=5, replica_groups=mesh['seg'=16,'samp'=2] {'seg','samp'}, dimensions={0}, use_global_device_ids=true | all-gather | bytes 67584 | tf_op jit(solution)/shard_map/all_gather | solution.py:12
  (264 shorter events, 78.3 us)
Async XLA Ops:
  0.6 5.0 copy-start
  0.6 8.2 %copy-start.1 = (bf16[32,128,128]{2,1,0:T(8,128)(2,1)S(1)}, bf16[32,128,128]{2,1,0:T(8,128)(2,1)}, u32[]{:S(2)}) copy-start(bf16[32,128,128]{2,1,0:T(8,128)(2,1)} %param.28) | copy-start | bytes 3145732
  0.7 10.6 %collective-permute-start = (bf16[32,1,128]{2,0,1:T(8,128)(2,1)S(1)}, bf16[32,1,128]{2,0,1:T(8,128)(2,1)S(1)}, u32[]{:S(2)}, u32[]{:S(2)}) collective-permute-start(bf16[32,1,128]{2,0,1:T(8,128)(2,1)S(1)} %slice.302), channel_id=1, source_target_pairs={{0,2},{2,4},{4,6},{6,8},{8,10},{10,12},{12,14},{14,16},{16,18},{18... | collective-permute-start | bytes 24584 | tf_op jit(solution)/shard_map/ppermute | solution.py:23
  6.1 5.7 %collective-permute-start.1 = (bf16[32,1,128]{2,0,1:T(8,128)(2,1)S(1)}, bf16[32,1,128]{2,0,1:T(8,128)(2,1)S(1)}, u32[]{:S(2)}, u32[]{:S(2)}) collective-permute-start(bf16[32,1,128]{2,0,1:T(8,128)(2,1)S(1)} %slice.366), channel_id=1, source_target_pairs={{2,0},{4,2},{6,4},{8,6},{10,8},{12,10},{14,12},{16,14},{18,16},{20... | collective-permute-start | bytes 24584 | tf_op jit(solution)/shard_map/ppermute | solution.py:23
  14.3 53.4 %copy-start.7 = (bf16[32,32,128]{2,0,1:T(8,128)(2,1)}, bf16[32,32,128]{2,0,1:T(8,128)(2,1)S(1)}, u32[]{:S(2)}) copy-start(bf16[32,32,128]{2,0,1:T(8,128)(2,1)S(1)} %convert_bitcast_fusion) | copy-start | bytes 786436
  17.6 50.2 %collective-permute-start.2 = (bf16[32,1,128]{2,0,1:T(8,128)(2,1)}, bf16[32,1,128]{2,0,1:T(8,128)(2,1)}, u32[]{:S(2)}, u32[]{:S(2)}) collective-permute-start(bf16[32,1,128]{2,0,1:T(8,128)(2,1)} %get-tuple-element.125), channel_id=1, source_target_pairs={{0,2},{2,4},{4,6},{6,8},{8,10},{10,12},{12,14},{14,16},{16,18},{18... | collective-permute-start | bytes 24584 | tf_op jit(solution)/shard_map/ppermute | solution.py:23
  66.2 5.7 %collective-permute-start.3 = (bf16[32,1,128]{2,0,1:T(8,128)(2,1)S(1)}, bf16[32,1,128]{2,0,1:T(8,128)(2,1)S(1)}, u32[]{:S(2)}, u32[]{:S(2)}) collective-permute-start(bf16[32,1,128]{2,0,1:T(8,128)(2,1)S(1)} %slice.371), channel_id=1, source_target_pairs={{2,0},{4,2},{6,4},{8,6},{10,8},{12,10},{14,12},{16,14},{18,16},{20... | collective-permute-start | bytes 24584 | tf_op jit(solution)/shard_map/ppermute | solution.py:23
  67.7 4.2 copy-start.10
  67.8 5.5 copy-start.4
  67.8 5.5 copy-start.6
  79.2 86.7 %collective-permute-start.4 = (bf16[32,1,128]{2,0,1:T(8,128)(2,1)}, bf16[32,1,128]{2,0,1:T(8,128)(2,1)}, u32[]{:S(2)}, u32[]{:S(2)}) collective-permute-start(bf16[32,1,128]{2,0,1:T(8,128)(2,1)} %get-tuple-element.122), channel_id=1, source_target_pairs={{0,2},{2,4},{4,6},{6,8},{8,10},{10,12},{12,14},{14,16},{16,18},{18... | collective-permute-start | bytes 24584 | tf_op jit(solution)/shard_map/ppermute | solution.py:23
  123.1 42.8 %collective-permute-start.5 = (bf16[32,1,128]{2,0,1:T(8,128)(2,1)}, bf16[32,1,128]{2,0,1:T(8,128)(2,1)}, u32[]{:S(2)}, u32[]{:S(2)}) collective-permute-start(bf16[32,1,128]{2,0,1:T(8,128)(2,1)} %slice.377), channel_id=1, source_target_pairs={{2,0},{4,2},{6,4},{8,6},{10,8},{12,10},{14,12},{16,14},{18,16},{20... | collective-permute-start | bytes 24584 | tf_op jit(solution)/shard_map/ppermute | solution.py:23
  173.4 43.6 %collective-permute-start.6 = (bf16[32,1,128]{2,0,1:T(8,128)(2,1)}, bf16[32,1,128]{2,0,1:T(8,128)(2,1)S(1)}, u32[]{:S(2)}, u32[]{:S(2)}) collective-permute-start(bf16[32,1,128]{2,0,1:T(8,128)(2,1)} %get-tuple-element.119), channel_id=1, source_target_pairs={{0,2},{2,4},{4,6},{6,8},{8,10},{10,12},{12,14},{14,16},{16,18},{18... | collective-permute-start | bytes 24584 | tf_op jit(solution)/shard_map/ppermute | solution.py:23
  215.4 5.7 %collective-permute-start.7 = (bf16[32,1,128]{2,0,1:T(8,128)(2,1)S(1)}, bf16[32,1,128]{2,0,1:T(8,128)(2,1)S(1)}, u32[]{:S(2)}, u32[]{:S(2)}) collective-permute-start(bf16[32,1,128]{2,0,1:T(8,128)(2,1)S(1)} %slice.383), channel_id=1, source_target_pairs={{2,0},{4,2},{6,4},{8,6},{10,8},{12,10},{14,12},{16,14},{18,16},{20... | collective-permute-start | bytes 24584 | tf_op jit(solution)/shard_map/ppermute | solution.py:23
  217.0 4.8 copy-start.16
  217.0 4.8 copy-start.22
  217.0 4.8 copy-start.66
  228.4 89.4 %collective-permute-start.8 = (bf16[32,1,128]{2,0,1:T(8,128)(2,1)}, bf16[32,1,128]{2,0,1:T(8,128)(2,1)}, u32[]{:S(2)}, u32[]{:S(2)}) collective-permute-start(bf16[32,1,128]{2,0,1:T(8,128)(2,1)} %get-tuple-element.116), channel_id=1, source_target_pairs={{0,2},{2,4},{4,6},{6,8},{8,10},{10,12},{12,14},{14,16},{16,18},{18... | collective-permute-start | bytes 24584 | tf_op jit(solution)/shard_map/ppermute | solution.py:23
  275.1 42.7 %collective-permute-start.9 = (bf16[32,1,128]{2,0,1:T(8,128)(2,1)}, bf16[32,1,128]{2,0,1:T(8,128)(2,1)}, u32[]{:S(2)}, u32[]{:S(2)}) collective-permute-start(bf16[32,1,128]{2,0,1:T(8,128)(2,1)} %slice.389), channel_id=1, source_target_pairs={{2,0},{4,2},{6,4},{8,6},{10,8},{12,10},{14,12},{16,14},{18,16},{20... | collective-permute-start | bytes 24584 | tf_op jit(solution)/shard_map/ppermute | solution.py:23
  325.3 43.8 %collective-permute-start.10 = (bf16[32,1,128]{2,0,1:T(8,128)(2,1)}, bf16[32,1,128]{2,0,1:T(8,128)(2,1)S(1)}, u32[]{:S(2)}, u32[]{:S(2)}) collective-permute-start(bf16[32,1,128]{2,0,1:T(8,128)(2,1)} %get-tuple-element.113), channel_id=1, source_target_pairs={{0,2},{2,4},{4,6},{6,8},{8,10},{10,12},{12,14},{14,16},{16,18},{18... | collective-permute-start | bytes 24584 | tf_op jit(solution)/shard_map/ppermute | solution.py:23
  367.3 5.7 %collective-permute-start.11 = (bf16[32,1,128]{2,0,1:T(8,128)(2,1)S(1)}, bf16[32,1,128]{2,0,1:T(8,128)(2,1)S(1)}, u32[]{:S(2)}, u32[]{:S(2)}) collective-permute-start(bf16[32,1,128]{2,0,1:T(8,128)(2,1)S(1)} %slice.395), channel_id=1, source_target_pairs={{2,0},{4,2},{6,4},{8,6},{10,8},{12,10},{14,12},{16,14},{18,16},{20... | collective-permute-start | bytes 24584 | tf_op jit(solution)/shard_map/ppermute | solution.py:23
  369.0 4.6 copy-start.18
  369.0 4.6 copy-start.64
  369.1 4.6 copy-start.67
  380.2 89.4 %collective-permute-start.12 = (bf16[32,1,128]{2,0,1:T(8,128)(2,1)}, bf16[32,1,128]{2,0,1:T(8,128)(2,1)}, u32[]{:S(2)}, u32[]{:S(2)}) collective-permute-start(bf16[32,1,128]{2,0,1:T(8,128)(2,1)} %get-tuple-element.110), channel_id=1, source_target_pairs={{0,2},{2,4},{4,6},{6,8},{8,10},{10,12},{12,14},{14,16},{16,18},{18... | collective-permute-start | bytes 24584 | tf_op jit(solution)/shard_map/ppermute | solution.py:23
  426.9 42.7 %collective-permute-start.13 = (bf16[32,1,128]{2,0,1:T(8,128)(2,1)}, bf16[32,1,128]{2,0,1:T(8,128)(2,1)}, u32[]{:S(2)}, u32[]{:S(2)}) collective-permute-start(bf16[32,1,128]{2,0,1:T(8,128)(2,1)} %slice.401), channel_id=1, source_target_pairs={{2,0},{4,2},{6,4},{8,6},{10,8},{12,10},{14,12},{16,14},{18,16},{20... | collective-permute-start | bytes 24584 | tf_op jit(solution)/shard_map/ppermute | solution.py:23
  477.1 40.4 %collective-permute-start.14 = (bf16[32,1,128]{2,0,1:T(8,128)(2,1)}, bf16[32,1,128]{2,0,1:T(8,128)(2,1)S(1)}, u32[]{:S(2)}, u32[]{:S(2)}) collective-permute-start(bf16[32,1,128]{2,0,1:T(8,128)(2,1)} %get-tuple-element.107), channel_id=1, source_target_pairs={{0,2},{2,4},{4,6},{6,8},{8,10},{10,12},{12,14},{14,16},{16,18},{18... | collective-permute-start | bytes 24584 | tf_op jit(solution)/shard_map/ppermute | solution.py:23
  515.9 5.7 %collective-permute-start.15 = (bf16[32,1,128]{2,0,1:T(8,128)(2,1)S(1)}, bf16[32,1,128]{2,0,1:T(8,128)(2,1)S(1)}, u32[]{:S(2)}, u32[]{:S(2)}) collective-permute-start(bf16[32,1,128]{2,0,1:T(8,128)(2,1)S(1)} %slice.407), channel_id=1, source_target_pairs={{2,0},{4,2},{6,4},{8,6},{10,8},{12,10},{14,12},{16,14},{18,16},{20... | collective-permute-start | bytes 24584 | tf_op jit(solution)/shard_map/ppermute | solution.py:23
  517.4 4.2 copy-start.9
  517.5 4.8 copy-start.20
  517.5 4.8 copy-start.62
  517.5 4.8 copy-start.65
  (60 other events, 98.1 us)
